TPU v7x, 1024 devices: a whole 8x8x8 slice. The times are simulated.
1024 devices in a mesh: dp: 16 (over y_lo, z), expert: 64 (over x, y_hi, core).
Axes of the slice: x: 8, y: 8 (y_hi: 4, y_lo: 2; y = y_hi * 2 + y_lo), z: 8, core: 2. Of those that a mesh axis runs over, the one named last changes fastest.
Arguments:
- out_grad: bfloat16 [3072, 7168], P('expert', 'dp'), may hold values from -6 to 6
- gate_weight: float32 [3072, 8], P('expert'), may hold values from 0.05 to 0.5
- expert_ids: int32 [3072, 8], P('expert'), may hold values from 0 to 63, all different within a row; in each aligned block of 48 rows (0 to 47, 48 to 95, ...) at most 9 rows name the same one
- replicated: int32 [64], replicated, may hold values from 0 to 1, as said below
- down_weight: bfloat16 [64, 1024, 7168], P('expert', None, 'dp'), may hold values from -0.0625 to 0.0625
- pre_act: bfloat16 [64, 2, 576, 2048], P('expert', None, 'dp'), may hold values from -6 to 6
Outputs:
- grad_down: bfloat16 [64, 1024, 7168], P('expert', None, 'dp')
- grad_pre: bfloat16 [64, 2, 576, 2048], P('expert', None, 'dp')
Inputs may be any that keep to these rules, and one draw needn't show every extreme that they name: `expert_ids`: each row names 8 different experts; among the 48 rows of one device no expert is named more than 9 times, a bound that some block reaches. `replicated`: expert 0 always has a redundant slot; each other expert has one with chance one half.
All inputs are finite; a program needn't handle non-finite values.
Results may differ from a plain program's by a relative error of at most 0.018.
Values may be sent and summed in bfloat16 or wider, within the bound.
A program may use at most 32 MiB of HBM per device.

v0:
```python
import jax
import jax.numpy as jnp
from jax import lax
from jax.sharding import PartitionSpec as P


def passed_along(value, axis, steps):
    count = lax.axis_size(axis)
    pairs = [(source, (source + steps) % count) for source in range(count)]
    return lax.ppermute(value, axis, pairs)


def hidden_of(stored):
    width = stored.shape[-1] // 2
    gate_part = stored[..., :width].astype(jnp.float32)
    up_part = stored[..., width:].astype(jnp.float32)
    return (gate_part * jax.nn.sigmoid(gate_part) * up_part).astype(jnp.bfloat16)


def swiglu_back(hidden_grad, stored):
    width = stored.shape[-1] // 2
    gate_part = stored[..., :width].astype(jnp.float32)
    up_part = stored[..., width:].astype(jnp.float32)
    sigmoid_v = jax.nn.sigmoid(gate_part)
    gate_grad = hidden_grad * up_part * sigmoid_v * (1.0 + gate_part * (1.0 - sigmoid_v))
    up_grad = hidden_grad * gate_part * sigmoid_v
    return jnp.concatenate([gate_grad, up_grad], axis=-1).astype(jnp.bfloat16)


def on_device(out_grad, gate_weight, expert_ids, replicated, down_weight, pre_act):
    devices = lax.axis_size("expert")
    half_way = devices // 2
    myself = lax.axis_index("expert")
    shares = lax.axis_size("dp")
    tokens_here, choose = expert_ids.shape
    rows_share = pre_act.shape[2]
    all_rows = rows_share * shares
    capacity = all_rows // devices
    flat_ids = expert_ids.reshape(-1)
    experts_iota = jnp.arange(devices, dtype=jnp.int32)
    onehot = (flat_ids[:, None] == experts_iota[None, :]).astype(jnp.int32)
    position = jnp.sum(onehot * (jnp.cumsum(onehot, axis=0) - 1), axis=1)
    rep_of = jnp.sum(onehot * replicated[None, :], axis=1)
    diverted = (rep_of == 1) & (myself % 2 == 1)
    target_dev = jnp.where(diverted, (flat_ids + half_way) % devices, flat_ids)
    slot_index = diverted.astype(jnp.int32)
    target = slot_index * devices * capacity + target_dev * capacity + position
    placer = (
        jnp.arange(2 * devices * capacity, dtype=jnp.int32)[:, None] == target[None, :]
    ).astype(jnp.bfloat16)
    scaled = gate_weight[:, :, None] * out_grad.astype(jnp.float32)[:, None, :]
    routed = scaled.astype(jnp.bfloat16).reshape(tokens_here * choose, -1)
    outgoing = jnp.dot(placer, routed, preferred_element_type=jnp.float32).astype(jnp.bfloat16)
    outgoing = outgoing.reshape(2, devices, capacity, -1)
    arrived = lax.all_to_all(outgoing, "expert", split_axis=1, concat_axis=1, tiled=True).reshape(
        2, all_rows, -1
    )
    own_weight = down_weight[0]
    fetched = passed_along(own_weight, "expert", half_way)
    weights = jnp.stack([own_weight, fetched])
    partial_value = jnp.einsum("srd,sfd->srf", arrived, weights, preferred_element_type=jnp.float32)
    hidden = hidden_of(pre_act[0])
    gradients = jnp.einsum(
        "srf,srd->sfd",
        lax.all_gather(hidden, "dp", axis=1, tiled=True),
        arrived,
        preferred_element_type=jnp.float32,
    )
    summed = lax.psum_scatter(
        partial_value.astype(jnp.bfloat16), "dp", scatter_dimension=1, tiled=True
    ).astype(jnp.float32)
    grad_pre = swiglu_back(summed, pre_act[0])[None]
    returned = passed_along(gradients[1].astype(jnp.bfloat16), "expert", half_way).astype(
        jnp.float32
    )
    grad_down = (gradients[0] + returned).astype(jnp.bfloat16)[None]
    return (grad_down, grad_pre)


def solution(mesh):
    in_specs = (
        P("expert", "dp"),
        P("expert", None),
        P("expert", None),
        P(),
        P("expert", None, "dp"),
        P("expert", None, "dp", None),
    )
    out_specs = (P("expert", None, "dp"), P("expert", None, "dp", None))
    return jax.shard_map(
        on_device, mesh=mesh, in_specs=in_specs, out_specs=out_specs, check_vma=False
    )
```

profile of v0, /device:TPU:8, one launch (start us, length us, event | category | flops | bytes accessed | tf_op | source)
XLA Modules:
  0.0 402.6 jit_solution(4532128582639009170)
XLA Ops:
  7.2 0.8 copy.21
  7.9 0.1 eq.56
  8.0 0.1 eq.63
  8.1 0.8 copy.24
  8.9 0.1 mul.71
  9.0 0.9 reduce-window.6
  9.9 0.2 slice_reduce_fusion
  10.2 0.8 convert_element_type.56
  11.0 0.8 select_reduce_fusion
  11.8 0.9 convolution_convert_fusion
  12.7 0.8 copy.25
  13.5 0.6 reshape.100
  14.1 2.3 copy.26
  16.5 0.0 copy-start.1
  16.5 17.5 %all-to-all-start = ((bf16[2,64,9,448]{3,0,2,1:T(2,128)(2,1)}), bf16[2,64,9,448]{3,0,2,1:T(2,128)(2,1)S(1)}, u32[]{:S(2)}, u32[]{:S(2)}) async-start(bf16[2,64,9,448]{3,0,2,1:T(2,128)(2,1)} %copy.26), calls=%async_computation | async-start | bytes 2359296 | tf_op jit(solution)/shard_map/all_to_all | solution.py:55
  34.0 0.0 all-reduce.3.cloned.1.call-start
  34.0 0.0 copy-done.1
  34.1 2.3 collective-permute-start.1
  36.3 29.2 %all-to-all-done = bf16[2,64,9,448]{3,0,2,1:T(2,128)(2,1)S(1)} async-done(((bf16[2,64,9,448]{3,0,2,1:T(2,128)(2,1)}), bf16[2,64,9,448]{3,0,2,1:T(2,128)(2,1)S(1)}, u32[]{:S(2)}, u32[]{:S(2)}) %all-to-all-start) | async-done | bytes 1032224 | tf_op jit(solution)/shard_map/all_to_all | solution.py:55
  65.5 2.0 copy.28
  67.5 18.9 %collective-permute-done.1 = bf16[1024,448]{0,1:T(8,128)(2,1)} collective-permute-done((bf16[1024,448]{0,1:T(8,128)(2,1)S(1)}, bf16[1024,448]{0,1:T(8,128)(2,1)}, u32[]{:S(2)}, u32[]{:S(2)}) %collective-permute-start.1) | collective-permute-done | bytes 917536 | tf_op jit(solution)/shard_map/ppermute | solution.py:10
  86.4 2.6 convolution_convert_fusion.1
  89.1 3.8 copy.30
  92.9 0.0 copy-start
  92.9 0.0 all-reduce.3.cloned.1.call-update
  92.9 0.0 all-gather.2.cloned.1.call-start
  93.0 1.3 dynamic-slice
  94.9 176.7 %all-reduce.3.cloned.1.call-done = bf16[2,576,1024]{2,0,1:T(2,128)(2,1)} async-done(((bf16[2,576,1024]{2,0,1:T(2,128)(2,1)}), bf16[2,576,1024]{2,0,1:T(2,128)(2,1)}) %all-reduce.3.cloned.1.call-update) | async-done | bytes 2359312
  271.6 0.0 copy-done
  271.6 1.5 fusion.25
  273.1 1.9 fusion.24
  275.0 0.0 all-gather.2.cloned.1.call-update
  275.0 76.4 %all-gather.2.cloned.1.call-done = bf16[2,576,1024]{2,0,1:T(2,128)(2,1)} async-done(((bf16[2,36,1024]{2,0,1:T(2,128)(2,1)}), bf16[2,576,1024]{2,0,1:T(2,128)(2,1)}) %all-gather.2.cloned.1.call-update) | async-done | bytes 2359312 | tf_op jit(solution)/shard_map/all_gather | solution.py:65
  351.4 3.4 fusion
  354.8 0.1 fusion.8
  354.9 2.2 collective-permute-start
  357.1 1.0 pad_maximum_fusion
  358.1 36.4 %collective-permute-done = bf16[1024,448]{0,1:T(8,128)(2,1)S(1)} collective-permute-done((bf16[1024,448]{0,1:T(8,128)(2,1)S(1)}, bf16[1024,448]{0,1:T(8,128)(2,1)S(1)}, u32[]{:S(2)}, u32[]{:S(2)}) %collective-permute-start) | collective-permute-done | bytes 917536 | tf_op jit(solution)/shard_map/ppermute | solution.py:10
  394.5 1.3 fusion.7
  (3 shorter events, 0.1 us)
Async XLA Ops:
  16.5 17.6 %copy-start.1 = (bf16[1,1024,448]{1,2,0:T(8,128)(2,1)S(1)}, bf16[1,1024,448]{1,2,0:T(8,128)(2,1)}, u32[]{:S(2)}) copy-start(bf16[1,1024,448]{1,2,0:T(8,128)(2,1)} %param.10) | copy-start | bytes 2752516
  16.5 49.1 %all-to-all-start = ((bf16[2,64,9,448]{3,0,2,1:T(2,128)(2,1)}), bf16[2,64,9,448]{3,0,2,1:T(2,128)(2,1)S(1)}, u32[]{:S(2)}, u32[]{:S(2)}) async-start(bf16[2,64,9,448]{3,0,2,1:T(2,128)(2,1)} %copy.26), calls=%async_computation | async-start | bytes 2359296 | tf_op jit(solution)/shard_map/all_to_all | solution.py:55
  34.0 237.6 %all-reduce.3.cloned.1.call-start = ((), (), s32[]{:S(2)}) async-start(), calls=%async_computation.2 | async-start | bytes 4718592
  34.1 52.4 %collective-permute-start.1 = (bf16[1024,448]{0,1:T(8,128)(2,1)S(1)}, bf16[1024,448]{0,1:T(8,128)(2,1)}, u32[]{:S(2)}, u32[]{:S(2)}) collective-permute-start(bf16[1024,448]{0,1:T(8,128)(2,1)S(1)} %bitcast.48), channel_id=1, source_target_pairs={{0,32},{1,33},{2,34},{3,35},{4,36},{5,37},{6,38},{7,39},{8,40},{9,... | collective-permute-start | bytes 2752520 | tf_op jit(solution)/shard_map/ppermute | solution.py:10
  92.9 178.7 %copy-start = (bf16[1,2,36,2048]{3,1,2,0:T(2,128)(2,1)S(1)}, bf16[1,2,36,2048]{3,1,2,0:T(2,128)(2,1)}, u32[]{:S(2)}) copy-start(bf16[1,2,36,2048]{3,1,2,0:T(2,128)(2,1)} %param.11) | copy-start | bytes 884740
  92.9 258.5 %all-gather.2.cloned.1.call-start = ((), (), s32[]{:S(2)}) async-start(), calls=%async_computation.1 | async-start | bytes 2506752 | tf_op jit(solution)/shard_map/all_gather | solution.py:65
  354.9 39.6 %collective-permute-start = (bf16[1024,448]{0,1:T(8,128)(2,1)S(1)}, bf16[1024,448]{0,1:T(8,128)(2,1)S(1)}, u32[]{:S(2)}, u32[]{:S(2)}) collective-permute-start(bf16[1024,448]{0,1:T(8,128)(2,1)S(1)} %fusion.8), channel_id=1, source_target_pairs={{0,32},{1,33},{2,34},{3,35},{4,36},{5,37},{6,38},{7,39},{8,40},{9,... | collective-permute-start | bytes 2752520 | tf_op jit(solution)/shard_map/ppermute | solution.py:10
Sparse Core Ops, SparseCore 0:
  93.0 178.5 all-reduce.2
  275.1 76.2 all-gather.1
where the time goes:
time: 403 us
  waiting for transfers between devices  338 us (84%)
  starting transfers between devices  22.1 us (5%)
  between operations  14.8 us (4%)
  local copies, waits for them, and re-layouts  13 us (3%)
  other arithmetic  8.17 us (2%)
  matrix products  6.85 us (2%)
    unnamed x3, waiting for transfers between devices  177 us
    all_gather x1, waiting for transfers between devices, on_device(): lax.all_gather(hidden, 'dp', axis=1, tiled=True)  76.4 us
    ppermute x2, waiting for transfers between devices, passed_along(): return lax.ppermute(value, axis, pairs)  55.3 us
    all_to_all x1, waiting for transfers between devices, on_device(): lax.all_to_all(outgoing, 'expert', split_axis=1, concat_axis=1, tiled=True)  29.2 us
    all_to_all x1, starting transfers between devices, on_device(): lax.all_to_all(outgoing, 'expert', split_axis=1, concat_axis=1, tiled=True)  17.5 us
  transfers between devices with their start and end apart: 5, of which 5 were waited for; matrix products, arithmetic and copies ran while one was open for 1% of the time, Pallas kernels for 0%

commit v1 on v0

v1 whole, which is shorter than its diff:
```python
import jax
import jax.numpy as jnp
from jax import lax
from jax.sharding import PartitionSpec as P


def passed_along(value, axis, steps):
    count = lax.axis_size(axis)
    pairs = [(source, (source + steps) % count) for source in range(count)]
    return lax.ppermute(value, axis, pairs)


def hidden_of(stored):
    width = stored.shape[-1] // 2
    gate_part = stored[..., :width].astype(jnp.float32)
    up_part = stored[..., width:].astype(jnp.float32)
    return (gate_part * jax.nn.sigmoid(gate_part) * up_part).astype(jnp.bfloat16)


def swiglu_back(hidden_grad, stored):
    width = stored.shape[-1] // 2
    gate_part = stored[..., :width].astype(jnp.float32)
    up_part = stored[..., width:].astype(jnp.float32)
    sigmoid_v = jax.nn.sigmoid(gate_part)
    gate_grad = hidden_grad * up_part * sigmoid_v * (1.0 + gate_part * (1.0 - sigmoid_v))
    up_grad = hidden_grad * gate_part * sigmoid_v
    return jnp.concatenate([gate_grad, up_grad], axis=-1).astype(jnp.bfloat16)


def on_device(out_grad, gate_weight, expert_ids, replicated, down_weight, pre_act):
    devices = lax.axis_size("expert")
    half_way = devices // 2
    myself = lax.axis_index("expert")
    shares = lax.axis_size("dp")
    share = lax.axis_index("dp")
    tokens_here, choose = expert_ids.shape
    rows_share = pre_act.shape[2]
    all_rows = rows_share * shares
    capacity = all_rows // devices
    routes = tokens_here * choose

    source = (share * rows_share + jnp.arange(rows_share)) // capacity
    mine_replicated = replicated[myself] == 1
    moved = ((source % 2 == 1) & mine_replicated)[:, None]

    hidden = hidden_of(pre_act[0])
    theirs = passed_along(hidden[1], "expert", half_way)
    merged = jnp.where(moved, theirs, hidden[0])
    gathered = lax.all_gather(merged, "dp", axis=0, tiled=True)

    flat_ids = expert_ids.reshape(-1)
    onehot = (flat_ids[:, None] == jnp.arange(devices, dtype=jnp.int32)[None, :])
    order = jnp.arange(routes, dtype=jnp.int32)
    earlier = (order[None, :] < order[:, None]).astype(jnp.bfloat16)
    counts = jnp.dot(earlier, onehot.astype(jnp.bfloat16), preferred_element_type=jnp.float32)
    position = jnp.sum(jnp.where(onehot, counts, 0.0), axis=1).astype(jnp.int32)
    target = flat_ids * capacity + position
    placer = (
        jnp.arange(devices * capacity, dtype=jnp.int32)[:, None] == target[None, :]
    ).astype(jnp.bfloat16)
    scaled = gate_weight[:, :, None] * out_grad.astype(jnp.float32)[:, None, :]
    routed = scaled.astype(jnp.bfloat16).reshape(routes, -1)
    outgoing = jnp.dot(placer, routed, preferred_element_type=jnp.float32).astype(jnp.bfloat16)
    outgoing = outgoing.reshape(devices, capacity, -1)
    arrived = lax.all_to_all(outgoing, "expert", split_axis=0, concat_axis=0, tiled=True)
    arrived = arrived.reshape(all_rows, -1)

    partial_value = jnp.einsum(
        "rd,fd->rf", arrived, down_weight[0], preferred_element_type=jnp.float32
    ).astype(jnp.bfloat16)
    parts = lax.all_to_all(
        partial_value.reshape(shares, rows_share, -1), "dp", split_axis=0, concat_axis=0, tiled=True
    )
    summed = jnp.sum(parts.astype(jnp.float32), axis=0)
    elsewhere = passed_along(
        jnp.where(moved, summed, 0.0).astype(jnp.bfloat16), "expert", half_way
    ).astype(jnp.float32)
    slots = jnp.stack([jnp.where(moved, 0.0, summed), elsewhere])
    grad_pre = swiglu_back(slots, pre_act[0])[None]

    grad_down = jnp.einsum(
        "rf,rd->fd", gathered, arrived, preferred_element_type=jnp.float32
    ).astype(jnp.bfloat16)[None]
    return (grad_down, grad_pre)


def solution(mesh):
    in_specs = (
        P("expert", "dp"),
        P("expert", None),
        P("expert", None),
        P(),
        P("expert", None, "dp"),
        P("expert", None, "dp", None),
    )
    out_specs = (P("expert", None, "dp"), P("expert", None, "dp", None))
    return jax.shard_map(
        on_device, mesh=mesh, in_specs=in_specs, out_specs=out_specs, check_vma=False
    )
```

time: 403 us -> 203 us (0.50)
  the two profiles are of different devices: /device:TPU:8 before, /device:TPU:2 now
where the time goes in v1:
time: 203 us
  waiting for transfers between devices  117 us (58%)
  blocking collectives  35.7 us (18%)
  starting transfers between devices  20.3 us (10%)
  between operations  14.9 us (7%)
  local copies, waits for them, and re-layouts  9.11 us (4%)
  matrix products  3.5 us (2%)
  other arithmetic  2.25 us (1%)
    all_gather x1, waiting for transfers between devices, on_device(): gathered = lax.all_gather(merged, 'dp', axis=0, tiled=True)  70.7 us
    all_to_all x1, blocking collectives, on_device(): lax.all_to_all(outgoing, 'expert', split_axis=0, concat_axis=0, tiled=True)  35.7 us
    all_to_all x1, waiting for transfers between devices, on_device(): lax.all_to_all(partial_value.reshape(shares, rows_share, -1), 'dp', split...  31.5 us
    ppermute x2, waiting for transfers between devices, passed_along(): return lax.ppermute(value, axis, pairs)  15 us
    all_to_all x1, starting transfers between devices, on_device(): lax.all_to_all(partial_value.reshape(shares, rows_share, -1), 'dp', split...  13.9 us
    ppermute x2, starting transfers between devices, passed_along(): return lax.ppermute(value, axis, pairs)  6.31 us
    unnamed x13, local copies, waits for them, and re-layouts  6.24 us
  transfers between devices with their start and end apart: 4, of which 4 were waited for; matrix products, arithmetic and copies ran while one was open for 1% of the time, Pallas kernels for 0%

profile of v1, /device:TPU:2, one launch (start us, length us, event | category | flops | bytes accessed | tf_op | source)
XLA Modules:
  0.0 203.0 jit_solution(13056254960351979607)
XLA Ops:
  7.2 0.0 copy-start
  7.2 0.8 copy.26
  8.0 0.1 reshape.116
  8.1 0.2 fusion.1
  8.4 0.8 convert_element_type.56
  9.2 0.8 copy.27
  9.9 0.1 mul.60
  10.0 0.6 convolution_convert_fusion.2
  10.7 0.2 copy.28
  10.9 0.3 reshape.117
  11.2 1.0 reshape.123
  12.2 35.7 %all_to_all.10 = bf16[64,2,2016]{2,1,0:T(2,128)(2,1)S(1)} all-to-all(bf16[64,2,2016]{2,1,0:T(2,128)(2,1)S(1)} %reshape.123), channel_id=1, replica_groups=mesh['dp'=16,'expert'=64] {'expert'}, dimensions={0} | all-to-all | bytes 1032192 | tf_op jit(solution)/shard_map/all_to_all | solution.py:65
  47.9 1.1 reshape.124
  49.0 0.4 reshape.118
  49.4 0.0 copy-done
  49.4 0.8 convolution_convert_fusion
  50.2 1.2 reshape.119
  51.4 0.0 copy-start.1
  51.4 0.0 copy-start.2
  51.4 13.9 %all-to-all-start.1 = ((bf16[16,36,1024]{2,1,0:T(8,128)(2,1)}), bf16[16,36,1024]{2,1,0:T(8,128)(2,1)S(1)}, u32[]{:S(2)}, u32[]{:S(2)}) async-start(bf16[16,36,1024]{2,1,0:T(8,128)(2,1)} %reshape.119), calls=%async_computation.1 | async-start | bytes 2621440 | tf_op jit(solution)/shard_map/all_to_all | solution.py:71
  65.4 0.0 all-gather.3.cloned.1.call-start
  65.4 0.0 copy-done.1
  65.4 0.1 copy.31
  65.5 0.0 copy-done.2
  65.6 0.6 dynamic_slice.3
  66.8 31.5 %all-to-all-done.1 = bf16[16,36,1024]{2,1,0:T(8,128)(2,1)S(1)} async-done(((bf16[16,36,1024]{2,1,0:T(8,128)(2,1)}), bf16[16,36,1024]{2,1,0:T(8,128)(2,1)S(1)}, u32[]{:S(2)}, u32[]{:S(2)}) %all-to-all-start.1) | async-done | bytes 1179680 | tf_op jit(solution)/shard_map/all_to_all | solution.py:71
  98.3 0.3 convert_reduce_fusion
  98.6 0.1 select_convert_fusion
  98.7 3.5 %collective-permute-start.1 = (bf16[36,1024]{1,0:T(8,128)(2,1)S(1)}, bf16[36,1024]{1,0:T(8,128)(2,1)S(1)}, u32[]{:S(2)}, u32[]{:S(2)}) collective-permute-start(bf16[36,1024]{1,0:T(8,128)(2,1)S(1)} %select_convert_fusion), channel_id=1, source_target_pairs={{0,32},{1,33},{2,34},{3,35},{4,36},{5,37},{6,38},{7,39},{8,40},{9,... | collective-permute-start | bytes 221192 | tf_op jit(solution)/shard_map/ppermute | solution.py:10
  102.2 0.1 bitcast_select_fusion
  102.3 7.5 %collective-permute-done.1 = bf16[36,1024]{1,0:T(8,128)(2,1)S(1)} collective-permute-done((bf16[36,1024]{1,0:T(8,128)(2,1)S(1)}, bf16[36,1024]{1,0:T(8,128)(2,1)S(1)}, u32[]{:S(2)}, u32[]{:S(2)}) %collective-permute-start.1) | collective-permute-done | bytes 73760 | tf_op jit(solution)/shard_map/ppermute | solution.py:10
  109.8 0.2 fusion.19
  110.1 2.8 %collective-permute-start = (bf16[36,1024]{1,0:T(8,128)(2,1)S(1)}, bf16[36,1024]{1,0:T(8,128)(2,1)S(1)}, u32[]{:S(2)}, u32[]{:S(2)}) collective-permute-start(bf16[36,1024]{1,0:T(8,128)(2,1)S(1)} %slice_bitcast_fusion.1), channel_id=1, source_target_pairs={{0,32},{1,33},{2,34},{3,35},{4,36},{5,37},{6,38},{7,39},{8,40},{9,... | collective-permute-start | bytes 221192 | tf_op jit(solution)/shard_map/ppermute | solution.py:10
  112.8 7.5 %collective-permute-done = bf16[36,1024]{1,0:T(8,128)(2,1)S(1)} collective-permute-done((bf16[36,1024]{1,0:T(8,128)(2,1)S(1)}, bf16[36,1024]{1,0:T(8,128)(2,1)S(1)}, u32[]{:S(2)}, u32[]{:S(2)}) %collective-permute-start) | collective-permute-done | bytes 73760 | tf_op jit(solution)/shard_map/ppermute | solution.py:10
  120.4 0.7 fusion.21
  121.1 0.0 all-gather.3.cloned.1.call-update
  121.1 1.0 copy.29
  122.2 70.7 %all-gather.3.cloned.1.call-done = bf16[16,36,1024]{2,1,0:T(8,128)(2,1)} async-done(((bf16[1,36,1024]{2,1,0:T(8,128)(2,1)}), bf16[16,36,1024]{2,1,0:T(8,128)(2,1)}) %all-gather.3.cloned.1.call-update) | async-done | bytes 1179664 | tf_op jit(solution)/shard_map/all_gather | solution.py:49
  192.9 1.4 reshape.122
  194.3 1.9 fusion
  (5 shorter events, 0.1 us)
Async XLA Ops:
  7.2 42.3 %copy-start = (bf16[1,1024,448]{1,2,0:T(8,128)(2,1)S(1)}, bf16[1,1024,448]{1,2,0:T(8,128)(2,1)}, u32[]{:S(2)}) copy-start(bf16[1,1024,448]{1,2,0:T(8,128)(2,1)} %param.10) | copy-start | bytes 2752516
  51.4 14.0 %copy-start.1 = (bf16[1,2,36,2048]{3,1,2,0:T(2,128)(2,1)S(1)}, bf16[1,2,36,2048]{3,1,2,0:T(2,128)(2,1)}, u32[]{:S(2)}) copy-start(bf16[1,2,36,2048]{3,1,2,0:T(2,128)(2,1)} %param.11) | copy-start | bytes 884740
  51.4 14.1 %copy-start.2 = (s32[64]{0:T(128)S(1)}, s32[64]{0:T(128)}, u32[]{:S(2)}) copy-start(s32[64]{0:T(128)} %param.9) | copy-start | bytes 772
  51.4 46.9 %all-to-all-start.1 = ((bf16[16,36,1024]{2,1,0:T(8,128)(2,1)}), bf16[16,36,1024]{2,1,0:T(8,128)(2,1)S(1)}, u32[]{:S(2)}, u32[]{:S(2)}) async-start(bf16[16,36,1024]{2,1,0:T(8,128)(2,1)} %reshape.119), calls=%async_computation.1 | async-start | bytes 2621440 | tf_op jit(solution)/shard_map/all_to_all | solution.py:71
  65.4 127.5 %all-gather.3.cloned.1.call-start = ((), (), s32[]{:S(2)}) async-start(), calls=%async_computation.2 | async-start | bytes 1392640 | tf_op jit(solution)/shard_map/all_gather | solution.py:49
  98.7 11.1 %collective-permute-start.1 = (bf16[36,1024]{1,0:T(8,128)(2,1)S(1)}, bf16[36,1024]{1,0:T(8,128)(2,1)S(1)}, u32[]{:S(2)}, u32[]{:S(2)}) collective-permute-start(bf16[36,1024]{1,0:T(8,128)(2,1)S(1)} %select_convert_fusion), channel_id=1, source_target_pairs={{0,32},{1,33},{2,34},{3,35},{4,36},{5,37},{6,38},{7,39},{8,40},{9,... | collective-permute-start | bytes 221192 | tf_op jit(solution)/shard_map/ppermute | solution.py:10
  110.1 10.3 %collective-permute-start = (bf16[36,1024]{1,0:T(8,128)(2,1)S(1)}, bf16[36,1024]{1,0:T(8,128)(2,1)S(1)}, u32[]{:S(2)}, u32[]{:S(2)}) collective-permute-start(bf16[36,1024]{1,0:T(8,128)(2,1)S(1)} %slice_bitcast_fusion.1), channel_id=1, source_target_pairs={{0,32},{1,33},{2,34},{3,35},{4,36},{5,37},{6,38},{7,39},{8,40},{9,... | collective-permute-start | bytes 221192 | tf_op jit(solution)/shard_map/ppermute | solution.py:10
Sparse Core Ops, SparseCore 0:
  121.2 71.6 all-gather.2

commit v2 on v0

v2 whole, which is shorter than its diff:
```python
import functools

import jax
import jax.numpy as jnp
import numpy as np
from jax import lax
from jax.experimental import pallas as pl
from jax.experimental.pallas import tpu as pltpu
from jax.sharding import PartitionSpec as P

F32, BF16 = jnp.float32, jnp.bfloat16
CAP = 9
LANES = 128


def up_to(value, step):
    return -(-value // step) * step


class Sizes:
    def __init__(self, mesh):
        self.dp, self.experts = mesh.shape["dp"], mesh.shape["expert"]
        self.nz = self.dp // 2
        self.nx = self.nz
        self.ny = self.experts // (2 * self.nx)
        self.slab = 2 * self.ny
        self.per_share = self.experts // self.dp
        self.share_rows = self.per_share * CAP
        self.half = up_to(self.share_rows, 8)
        self.rows = 2 * self.half


def row_wants(z, tokens):
    wants = np.full((z.rows, z.slab * tokens), -1.0, np.float32)
    for h in range(2):
        for u in range(z.share_rows):
            source = h * z.per_share + u // CAP
            wants[h * z.half + u, source * tokens : (source + 1) * tokens] = u % CAP + 1
    return wants


def stacked(value):
    width = value.shape[1] // 2
    return jnp.concatenate([value[:, :width], value[:, width:]], axis=0)


def kernel(
    z,
    g_ref, hid_ref, moved_ref, wants_ref, wt_ref,
    gd_ref, hg_ref,
    gall, theirs, hbuf, hall, dsend, dbuf, pbuf, prec, ssend, zrec, fsend, frec,
    gy_s, gy_r, gc_s, gc_r, th_s, th_r, hz_s, hz_r, hy_s, hy_r,
    dx_s, dx_r, py_s, py_r, rz_s, rz_r, fx_s, fx_r,
):
    dp, ex = lax.axis_index("dp"), lax.axis_index("expert")
    y_lo, my_z = dp // z.nz, dp % z.nz
    my_x, yc = ex // z.slab, ex % z.slab
    y_hi, core = yc // 2, yc % 2

    def at_z(k):
        return y_lo * z.nz + (my_z + k) % z.nz

    def at_x(k):
        return ((my_x + k) % z.nx) * z.slab + yc

    def in_slab(k):
        return ((y_hi + k) % z.ny) * 2 + core

    def at_y(k):
        return my_x * z.slab + in_slab(k)

    other = (1 - y_lo) * z.nz + my_z
    sibling = my_x * z.slab + y_hi * 2 + 1 - core
    opposite = at_x(z.nx // 2)

    def send(src, dst, s, r, **where):
        copy = pltpu.make_async_remote_copy(
            src_ref=src, dst_ref=dst, send_sem=s, recv_sem=r,
            device_id=where, device_id_type=pl.DeviceIdType.MESH,
        )
        return copy

    barrier = pltpu.get_barrier_semaphore()
    greeted = (
        [dict(dp=at_z(k)) for k in range(1, z.nz)]
        + [dict(dp=other)]
        + [dict(expert=at_x(k)) for k in range(1, z.nx)]
        + [dict(expert=at_y(k)) for k in range(1, z.ny)]
        + [dict(expert=sibling)]
    )
    for where in greeted:
        pl.semaphore_signal(barrier, inc=1, device_id=where, device_id_type=pl.DeviceIdType.MESH)
    pl.semaphore_wait(barrier, len(greeted))

    to_y = [
        send(g_ref, gall.at[yc], gy_s.at[k], gy_r.at[k], expert=at_y(k)) for k in range(1, z.ny)
    ]
    for copy in to_y:
        copy.start()
    to_core = [send(g_ref, gall.at[yc], gc_s.at[0], gc_r.at[0], expert=sibling)]
    to_core[0].start()
    to_partner = send(hid_ref.at[1], theirs, th_s, th_r, expert=opposite)
    to_partner.start()
    gall[yc] = g_ref[...]

    moved = jnp.concatenate([moved_ref[...]] * (hbuf.shape[2] // LANES), axis=1)
    to_partner.wait_recv()
    hbuf[dp] = (
        hid_ref[0].astype(F32) * (1.0 - moved) + theirs[...].astype(F32) * moved
    ).astype(BF16)
    to_z = [
        send(hbuf.at[dp], hbuf.at[dp], hz_s.at[k], hz_r.at[k], dp=at_z(k)) for k in range(1, z.nz)
    ]
    for copy in to_z:
        copy.start()
    to_other = [send(hbuf.at[dp], hbuf.at[dp], hy_s.at[0], hy_r.at[0], dp=other)]
    to_other[0].start()

    for k in range(1, z.ny):
        to_y[k - 1].wait_recv()
        slot = in_slab(z.ny - k)
        copy = send(gall.at[slot], gall.at[slot], gc_s.at[k], gc_r.at[k], expert=sibling)
        copy.start()
        to_core.append(copy)
    for copy in to_core:
        copy.wait_recv()

    tokens = g_ref.shape[0]
    width = wt_ref.shape[0]
    data = gall[...].reshape(z.slab * tokens, g_ref.shape[1])
    table = up_to(width + z.experts, LANES)
    first = table - LANES
    places = data[:, first:table]
    lane = lax.broadcasted_iota(jnp.int32, (z.rows, LANES), 1)
    wants = wants_ref[...]
    to_x = []
    for k in list(range(z.nx // 2, 0, -1)) + [0]:
        for step in (k,) if k in (0, z.nx // 2) else (k, z.nx - k):
            expert = at_x(step)
            chosen = jnp.where(lane == width - first + expert, 1.0, 0.0).astype(BF16)
            ranks = lax.dot_general(
                chosen, places, (((1,), (1,)), ((), ())), preferred_element_type=F32
            )
            picker = jnp.where(ranks == wants, 1.0, 0.0).astype(BF16)
            picked = jnp.dot(picker, data, preferred_element_type=F32)
            about = picked[:, table : table + LANES]
            named = jnp.where((lane < 8) & (about == expert.astype(F32)), 1.0, 0.0)
            parts = sum(pltpu.roll(named, 8 * n, 1) for n in (1, 2, 3))
            weight = jnp.sum(about * parts, axis=1, keepdims=True)
            rows = (picked[:, :table] * weight).astype(BF16)
            if step == 0:
                dbuf[my_x] = rows
            else:
                dsend[step] = rows
                copy = send(
                    dsend.at[step], dbuf.at[my_x], dx_s.at[step], dx_r.at[step], expert=expert
                )
                copy.start()
                to_x.append(copy)

    for k in range(1, z.nz):
        to_z[k - 1].wait_recv()
        slot = at_z(z.nz - k)
        copy = send(hbuf.at[slot], hbuf.at[slot], hy_s.at[k], hy_r.at[k], dp=other)
        copy.start()
        to_other.append(copy)

    per_half = z.nx // 2
    for k in range(0, z.nx // 2 + 1):
        for step in (k,) if k in (0, z.nx // 2) else (z.nx - k, k):
            slab = (my_x + step) % z.nx
            if step:
                back = z.nx - step
                send(
                    dsend.at[back], dbuf.at[slab], dx_s.at[back], dx_r.at[back], expert=at_x(back)
                ).wait_recv()
            part = jnp.dot(dbuf[slab][:, :width], wt_ref[...], preferred_element_type=F32)
            for h in range(2):
                pbuf[slab, h] = stacked(part[h * z.half : (h + 1) * z.half]).astype(BF16)

            @pl.when(slab // per_half != y_lo)
            def _():
                q = slab % per_half
                send(pbuf.at[slab], prec.at[q], py_s.at[q], py_r.at[q], dp=other).start()

    for q in range(per_half):
        send(pbuf.at[q], prec.at[q], py_s.at[q], py_r.at[q], dp=other).wait_recv()
        for h in range(2):
            both = pbuf[y_lo * per_half + q, h].astype(F32) + prec[q, h].astype(F32)
            to = 2 * q + h
            ssend[to] = both.astype(BF16)

            @pl.when(to != my_z)
            def _():
                k = (to - my_z + z.nz) % z.nz
                send(
                    ssend.at[to], zrec.at[my_z], rz_s.at[k], rz_r.at[k], dp=y_lo * z.nz + to
                ).start()

    for copy in to_other:
        copy.wait_recv()
    for slab in range(z.nx):
        pair = [hbuf[2 * slab + h].astype(F32) for h in range(2)]
        for side in range(2):
            piece = jnp.concatenate([p[side * z.half : (side + 1) * z.half] for p in pair], axis=0)
            hall[slab, :, side * piece.shape[1] : (side + 1) * piece.shape[1]] = piece.astype(BF16)
    rows_all = dbuf[...].reshape(z.nx * z.rows, dbuf.shape[2])
    tile = min(256, gd_ref.shape[1])

    def columns(n, carry):
        at = pl.ds(pl.multiple_of(n * tile, tile), tile)
        kept = hall[:, :, at].reshape(z.nx * z.rows, tile)
        full = lax.dot_general(
            rows_all, kept, (((0,), (0,)), ((), ())), preferred_element_type=F32
        )
        gd_ref[:, at] = full[:width].astype(BF16)
        return carry

    lax.fori_loop(0, gd_ref.shape[1] // tile, columns, 0)

    total = ssend[my_z].astype(F32)
    for k in range(1, z.nz):
        back = z.nz - k
        send(ssend.at[0], zrec.at[0], rz_s.at[k], rz_r.at[k], dp=at_z(k)).wait_recv()
        total = total + zrec[(my_z + back) % z.nz].astype(F32)
    fsend[...] = (total * moved).astype(BF16)
    last = send(fsend, frec, fx_s, fx_r, expert=opposite)
    last.start()
    hg_ref[0] = total * (1.0 - moved)
    last.wait_recv()
    hg_ref[1] = frec[...].astype(F32)

    for copy in to_y + to_core + [to_partner] + to_z + to_other + to_x + [last]:
        copy.wait_send()
    for q in range(per_half):
        send(pbuf.at[q], prec.at[q], py_s.at[q], py_r.at[q], dp=other).wait_send()
    for k in range(1, z.nz):
        send(ssend.at[0], zrec.at[0], rz_s.at[k], rz_r.at[k], dp=at_z(k)).wait_send()


def hidden_of(stored):
    width = stored.shape[-1] // 2
    gate_part = stored[..., :width].astype(F32)
    up_part = stored[..., width:].astype(F32)
    return (gate_part * jax.nn.sigmoid(gate_part) * up_part).astype(BF16)


def swiglu_back(hidden_grad, stored):
    width = stored.shape[-1] // 2
    gate_part = stored[..., :width].astype(F32)
    up_part = stored[..., width:].astype(F32)
    sigmoid_v = jax.nn.sigmoid(gate_part)
    gate_grad = hidden_grad * up_part * sigmoid_v * (1.0 + gate_part * (1.0 - sigmoid_v))
    up_grad = hidden_grad * gate_part * sigmoid_v
    return jnp.concatenate([gate_grad, up_grad], axis=-1).astype(BF16)


def on_device(z, out_grad, gate_weight, expert_ids, replicated, down_weight, pre_act):
    tokens, width = out_grad.shape
    hidden_width = pre_act.shape[3] // 2
    half_lanes = hidden_width // 2
    share, myself = lax.axis_index("dp"), lax.axis_index("expert")

    experts = jnp.arange(z.experts, dtype=jnp.int32)
    named = jnp.any(expert_ids[:, :, None] == experts, axis=1)
    order = jnp.arange(tokens)
    earlier = (order[None, :] < order[:, None]).astype(BF16)
    ranks = 1.0 + jnp.dot(earlier, named.astype(BF16), preferred_element_type=F32)
    ranks = jnp.where(named, ranks, 0.0).astype(BF16)
    high = lax.reduce_precision(gate_weight, 8, 7)
    middle = lax.reduce_precision(gate_weight - high, 8, 7)
    low = gate_weight - high - middle
    table = up_to(width + z.experts, LANES)
    about = jnp.concatenate([expert_ids.astype(F32), high, middle, low], axis=1).astype(BF16)
    fill = jnp.zeros((tokens, table - width - z.experts), BF16)
    message = jnp.concatenate([out_grad, ranks, fill, about], axis=1)
    message = jnp.pad(message, ((0, 0), (0, table + LANES - message.shape[1])))

    hidden = jnp.pad(hidden_of(pre_act[0]), ((0, 0), (0, z.half - z.share_rows), (0, 0)))
    hidden = hidden.reshape(2, z.half, 2, half_lanes).swapaxes(1, 2).reshape(2, z.rows, half_lanes)
    inside = jnp.arange(z.rows) % z.half
    source = share * z.per_share + inside // CAP
    moved = (source % 2 == 1) & (inside < z.share_rows) & (replicated[myself] == 1)
    moved = jnp.broadcast_to(moved.astype(F32)[:, None], (z.rows, LANES))
    weight = jnp.swapaxes(down_weight[0], 0, 1)
    wants = jnp.asarray(row_wants(z, tokens))

    chunk = (z.rows, half_lanes)
    dma = pltpu.SemaphoreType.DMA
    gd, hg = pl.pallas_call(
        functools.partial(kernel, z),
        out_shape=(
            jax.ShapeDtypeStruct((width, hidden_width), BF16),
            jax.ShapeDtypeStruct((2,) + chunk, F32),
        ),
        in_specs=[pl.BlockSpec(memory_space=pltpu.VMEM)] * 5,
        out_specs=(pl.BlockSpec(memory_space=pltpu.VMEM),) * 2,
        scratch_shapes=[
            pltpu.VMEM((z.slab, tokens, table + LANES), BF16),
            pltpu.VMEM(chunk, BF16),
            pltpu.VMEM((z.dp,) + chunk, BF16),
            pltpu.VMEM((z.nx, z.rows, hidden_width), BF16),
            pltpu.VMEM((z.nx, z.rows, table), BF16),
            pltpu.VMEM((z.nx, z.rows, table), BF16),
            pltpu.VMEM((z.nx, 2) + chunk, BF16),
            pltpu.VMEM((z.nx // 2, 2) + chunk, BF16),
            pltpu.VMEM((z.nz,) + chunk, BF16),
            pltpu.VMEM((z.nz,) + chunk, BF16),
            pltpu.VMEM(chunk, BF16),
            pltpu.VMEM(chunk, BF16),
            dma((max(z.ny, 2),)), dma((max(z.ny, 2),)), dma((z.ny,)), dma((z.ny,)), dma, dma,
            dma((z.nz,)), dma((z.nz,)), dma((z.nz,)), dma((z.nz,)),
            dma((z.nx,)), dma((z.nx,)), dma((z.nx // 2,)), dma((z.nx // 2,)),
            dma((z.nz,)), dma((z.nz,)), dma, dma,
        ],
        compiler_params=pltpu.CompilerParams(
            collective_id=0, has_side_effects=True, vmem_limit_bytes=40 << 20
        ),
    )(message, hidden, moved, wants, weight)

    hg = hg.reshape(2, 2, z.half, half_lanes)[:, :, : z.share_rows]
    hg = hg.swapaxes(1, 2).reshape(2, z.share_rows, hidden_width)
    return (jnp.swapaxes(gd, 0, 1)[None], swiglu_back(hg, pre_act[0])[None])


def solution(mesh):
    in_specs = (
        P("expert", "dp"),
        P("expert", None),
        P("expert", None),
        P(),
        P("expert", None, "dp"),
        P("expert", None, "dp", None),
    )
    out_specs = (P("expert", None, "dp"), P("expert", None, "dp", None))
    return jax.shard_map(
        functools.partial(on_device, Sizes(mesh)),
        mesh=mesh, in_specs=in_specs, out_specs=out_specs, check_vma=False,
    )
```

time: 403 us -> 91.1 us (0.23)
  the two profiles are of different devices: /device:TPU:8 before, /device:TPU:128 now
where the time goes in v2:
time: 91.1 us; the launch traced here: 90.8 us
  Pallas kernels  82 us (90%)
  local copies, waits for them, and re-layouts  5.21 us (6%)
  other arithmetic  2 us (2%)
  between operations  1.43 us (2%)
    pallas_call x1, Pallas kernels, on_device(): pl.pallas_call(functools.partial(kernel, z), out_shape=(jax.ShapeDtypeStr...  82 us
    unnamed x17, local copies, waits for them, and re-layouts  3.3 us

profile of v2, /device:TPU:128, one launch (start us, length us, event | category | flops | bytes accessed | tf_op | source)
XLA Modules:
  0.0 90.8 jit_solution(15871453651943638685)
XLA Ops:
  0.6 0.0 copy-start.6
  0.6 0.6 copy-done.6
  1.3 0.6 dynamic_slice.3
  2.5 0.0 copy-start.4
  2.6 0.0 copy-start.5
  2.6 0.0 copy-start.3
  2.6 0.1 broadcast_in_dim.9.moved_ref
  2.7 0.6 copy-done.4
  3.2 0.0 copy-start.2
  3.2 0.1 copy.23
  3.3 0.1 copy.22
  3.4 0.1 copy.25
  3.5 0.0 copy-done.5
  3.5 0.1 copy.21
  3.6 0.2 fusion.12
  3.7 0.1 fusion.1
  3.9 0.1 copy.24
  4.0 0.0 copy-done.3
  4.0 0.1 concatenate.21
  4.1 0.0 copy-start
  4.1 0.1 copy-done.2
  4.2 0.4 fusion.2
  4.5 0.1 pad.9
  4.7 0.1 reshape.84
  4.8 0.0 copy-start.1
  4.8 0.4 copy-done
  5.3 0.5 copy-done.1
  5.8 82.0 %shard_map.86 = (bf16[448,1024]{1,0:T(8,128)(2,1)S(1)}, f32[2,80,512]{2,1,0:T(8,128)S(1)}) custom-call(bf16[48,640]{1,0:T(8,128)(2,1)S(1)} %pad.8.g_ref, bf16[2,80,512]{2,1,0:T(8,128)(2,1)S(1)} %bitcast.25, f32[80,128]{1,0:T(8,128)S(1)} %broadcast_in_dim.9.moved_ref, f32[80,384]{1,0:T(8,128)S(1)} %copy-done.1, bf16[448,1024]{1,0:T(8,128)(2,1)S(1)} %bitcast.23), custom_call_target="tpu_custom_call" | custom-call | tf_op jit(solution)/shard_map/pallas_call | solution.py:290
  87.8 0.2 copy.27
  88.1 0.4 reshape.87
  88.4 0.5 fusion.14
  88.9 1.0 %pad_maximum_fusion = bf16[1,2,36,2048]{3,1,2,0:T(2,128)(2,1)} fusion(bf16[1,2,36,1024]{3,1,2,0:T(2,128)(2,1)S(1)} %get-tuple-element.9, bf16[1,2,36,1024]{3,1,2,0:T(2,128)(2,1)S(1)} %get-tuple-element.8), kind=kLoop, calls=%fused_computation.20 | loop fusion | flops 589824 | bytes 589824 | tf_op jit(solution)/shard_map/concatenate | solution.py:255
  89.9 0.9 %copy.29 = bf16[1,1024,448]{1,2,0:T(8,128)(2,1)} copy(bf16[1,1024,448]{1,2,0:T(8,128)(2,1)S(1)} %bitcast.24) | data formatting | bytes 1835008
  (7 shorter events, 0.1 us)
Async XLA Ops:
  0.6 0.7 copy-start.6
  2.5 0.7 copy-start.4
  2.6 0.9 %copy-start.5 = (s32[48,8]{0,1:T(8,128)S(1)}, s32[48,8]{0,1:T(8,128)}, u32[]{:S(2)}) copy-start(s32[48,8]{0,1:T(8,128)} %param.9) | copy-start | bytes 4612
  2.6 1.4 %copy-start.3 = (bf16[48,448]{1,0:T(8,128)(2,1)S(1)}, bf16[48,448]{1,0:T(8,128)(2,1)}, u32[]{:S(2)}) copy-start(bf16[48,448]{1,0:T(8,128)(2,1)} %param.7) | copy-start | bytes 129028
  3.2 1.0 %copy-start.2 = (bf16[1,2,36,2048]{3,1,2,0:T(2,128)(2,1)S(1)}, bf16[1,2,36,2048]{3,1,2,0:T(2,128)(2,1)}, u32[]{:S(2)}) copy-start(bf16[1,2,36,2048]{3,1,2,0:T(2,128)(2,1)} %param.12) | copy-start | bytes 884740
  4.1 1.2 %copy-start = (bf16[1,1024,448]{1,2,0:T(8,128)(2,1)S(1)}, bf16[1,1024,448]{1,2,0:T(8,128)(2,1)}, u32[]{:S(2)}) copy-start(bf16[1,1024,448]{1,2,0:T(8,128)(2,1)} %param.11) | copy-start | bytes 2752516
  4.8 1.0 %copy-start.1 = (f32[80,384]{1,0:T(8,128)S(1)}, f32[80,384]{1,0:T(8,128)}, u32[]{:S(2)}) copy-start(f32[80,384]{1,0:T(8,128)} %constant.63.clone.wants_ref) | copy-start | bytes 368644

commit v3 on v2

v3 whole, which is shorter than its diff:
```python
import functools

import jax
import jax.numpy as jnp
import numpy as np
from jax import lax
from jax.experimental import pallas as pl
from jax.experimental.pallas import tpu as pltpu
from jax.sharding import PartitionSpec as P

F32, BF16 = jnp.float32, jnp.bfloat16
CAP = 9
LANES = 128


def up_to(value, step):
    return -(-value // step) * step


class Sizes:
    def __init__(self, mesh):
        self.dp, self.experts = mesh.shape["dp"], mesh.shape["expert"]
        self.nz = self.dp // 2
        self.nx = self.nz
        self.ny = self.experts // (2 * self.nx)
        self.slab = 2 * self.ny
        self.per_share = self.experts // self.dp
        self.share_rows = self.per_share * CAP
        self.half = up_to(self.share_rows, 8)
        self.rows = 2 * self.half


def share_order(z):
    return list(range(1, z.per_share, 2)) + list(range(0, z.per_share, 2))


def packing(width):
    blocks = width // LANES
    return blocks, up_to(blocks * CAP + (CAP + 1) // 2, 16)


def packed_wants(tokens, width):
    blocks, rows = packing(width)
    wants = np.full((rows, up_to((blocks + 2) * tokens, LANES)), -1.0, np.float32)
    for r in range(CAP):
        for b in range(blocks):
            wants[b * CAP + r, b * tokens : (b + 1) * tokens] = r + 1
        side = blocks + r % 2
        wants[blocks * CAP + r // 2, side * tokens : (side + 1) * tokens] = r + 1
    return wants


def unpacking(z, width):
    blocks, rows = packing(width)
    taken = np.zeros((blocks + 2, z.rows, z.slab * rows), np.float32)
    for h in range(2):
        for n, source in enumerate(share_order(z)):
            for r in range(CAP):
                at, start = h * z.half + n * CAP + r, (h * z.per_share + source) * rows
                for b in range(blocks):
                    taken[b, at, start + b * CAP + r] = 1
                taken[blocks + r % 2, at, start + blocks * CAP + r // 2] = 1
    return taken.reshape(-1, z.slab * rows)


def stacked(value):
    width = value.shape[1] // 2
    return jnp.concatenate([value[:, :width], value[:, width:]], axis=0)


def kernel(
    z,
    tok_ref, tab_ref, hid_ref, moved_ref, wants_ref, take_ref, wt_ref,
    gd_ref, hg_ref,
    sbuf, abuf, theirs, hbuf, hall, dbuf, pbuf, prec, ssend, zrec, fsend, frec,
    th_s, th_r, hz_s, hz_r, hy_s, hy_r,
    dx_s, dx_r, py_s, py_r, rz_s, rz_r, fx_s, fx_r,
):
    dp, ex = lax.axis_index("dp"), lax.axis_index("expert")
    y_lo, my_z = dp // z.nz, dp % z.nz
    my_x, yc = ex // z.slab, ex % z.slab

    def at_z(k):
        return y_lo * z.nz + (my_z + k) % z.nz

    def at_x(k):
        return ((my_x + k) % z.nx) * z.slab + yc

    other = (1 - y_lo) * z.nz + my_z
    opposite = at_x(z.nx // 2)

    def send(src, dst, s, r, **where):
        copy = pltpu.make_async_remote_copy(
            src_ref=src, dst_ref=dst, send_sem=s, recv_sem=r,
            device_id=where, device_id_type=pl.DeviceIdType.MESH,
        )
        return copy

    barrier = pltpu.get_barrier_semaphore()
    def greet(**where):
        pl.semaphore_signal(barrier, inc=1, device_id=where, device_id_type=pl.DeviceIdType.MESH)

    def greet_expert(k, carry):
        greet(expert=(ex + k) % z.experts)
        return carry

    lax.fori_loop(1, z.experts, greet_expert, 0)
    for k in range(1, z.nz):
        greet(dp=at_z(k))
    greet(dp=other)
    pl.semaphore_wait(barrier, z.experts + z.nz - 1)

    to_partner = send(hid_ref.at[1], theirs, th_s, th_r, expert=opposite)
    to_partner.start()

    message = sbuf.shape[2:]
    width = wt_ref.shape[0]
    tokens, wants = tok_ref[...], wants_ref[...]

    def prepare(step):
        x = (my_x + step) % z.nx
        shape = (z.slab,) + wants.shape
        hit = jnp.broadcast_to(tab_ref[0, x][:, None], shape) == wants[None]
        picked = 0.0
        for n in range(1, 4):
            part = jnp.where(hit, jnp.broadcast_to(tab_ref[n, x][:, None], shape), 0.0)
            part = part.reshape(-1, shape[2]).astype(BF16)
            picked = picked + jnp.dot(part, tokens, preferred_element_type=F32)
        sbuf[step] = picked.astype(BF16).reshape(sbuf.shape[1:])
        return x

    def to_slab(n, carry):
        step = 1 + (n + z.nx // 2 - 1) % (z.nx - 1)
        x = prepare(step)

        def one(j, inner):
            send(
                sbuf.at[step, j], abuf.at[my_x, yc], dx_s.at[step], dx_r.at[step],
                expert=x * z.slab + j,
            ).start()
            return inner

        return lax.fori_loop(0, z.slab, one, carry)

    def to_own_slab(m, carry):
        j = (yc + m) % z.slab
        send(
            sbuf.at[0, j], abuf.at[my_x, yc], dx_s.at[0], dx_r.at[0], expert=my_x * z.slab + j
        ).start()
        return carry

    lax.fori_loop(0, z.nx - 1, to_slab, 0)
    prepare(0)
    lax.fori_loop(1, z.slab, to_own_slab, 0)
    abuf[my_x, yc] = sbuf[0, yc]

    moved = jnp.concatenate([moved_ref[...]] * (hbuf.shape[2] // LANES), axis=1)
    to_partner.wait_recv()
    hbuf[dp] = (
        hid_ref[0].astype(F32) * (1.0 - moved) + theirs[...].astype(F32) * moved
    ).astype(BF16)
    to_z = [
        send(hbuf.at[dp], hbuf.at[dp], hz_s.at[k], hz_r.at[k], dp=at_z(k)) for k in range(1, z.nz)
    ]
    for copy in to_z:
        copy.start()
    to_other = [send(hbuf.at[dp], hbuf.at[dp], hy_s.at[0], hy_r.at[0], dp=other)]
    to_other[0].start()

    per_half = z.nx // 2
    for k in range(0, z.nx // 2 + 1):
        for step in (k,) if k in (0, z.nx // 2) else (z.nx - k, k):
            slab = (my_x + step) % z.nx
            back = (z.nx - step) % z.nx
            came = abuf.at[slab] if step else abuf.at[slab, pl.ds(0, z.slab - 1)]
            send(came, came, dx_s.at[back], dx_r.at[back], dp=other).wait_recv()
            arrived = abuf[slab].reshape(z.slab * message[0], message[1])
            taken = jnp.dot(take_ref[...], arrived, preferred_element_type=F32)
            taken = [taken[n * z.rows : (n + 1) * z.rows] for n in range(taken.shape[0] // z.rows)]
            ends = taken[-2] + pltpu.roll(taken[-1], LANES // 2, 1)
            dbuf[slab] = jnp.concatenate(taken[:-2] + [ends], axis=1).astype(BF16)
            part = jnp.dot(dbuf[slab][:, :width], wt_ref[...], preferred_element_type=F32)
            for h in range(2):
                pbuf[slab, h] = stacked(part[h * z.half : (h + 1) * z.half]).astype(BF16)

            @pl.when(slab // per_half != y_lo)
            def _():
                q = slab % per_half
                send(pbuf.at[slab], prec.at[q], py_s.at[q], py_r.at[q], dp=other).start()

    for q in range(per_half):
        send(pbuf.at[q], prec.at[q], py_s.at[q], py_r.at[q], dp=other).wait_recv()
        for h in range(2):
            both = pbuf[y_lo * per_half + q, h].astype(F32) + prec[q, h].astype(F32)
            to = 2 * q + h
            ssend[to] = both.astype(BF16)

            @pl.when(to != my_z)
            def _():
                k = (to - my_z + z.nz) % z.nz
                send(
                    ssend.at[to], zrec.at[my_z], rz_s.at[k], rz_r.at[k], dp=y_lo * z.nz + to
                ).start()

    for k in range(1, z.nz):
        to_z[k - 1].wait_recv()
        slot = at_z(z.nz - k)
        copy = send(hbuf.at[slot], hbuf.at[slot], hy_s.at[k], hy_r.at[k], dp=other)
        copy.start()
        to_other.append(copy)

    total = ssend[my_z].astype(F32)
    for k in range(1, z.nz):
        back = z.nz - k
        send(ssend.at[0], zrec.at[0], rz_s.at[k], rz_r.at[k], dp=at_z(k)).wait_recv()
        total = total + zrec[(my_z + back) % z.nz].astype(F32)
    few = fsend.shape[0] // 2
    going = total * moved
    fsend[...] = jnp.concatenate([going[:few], going[z.half : z.half + few]], axis=0).astype(BF16)
    last = send(fsend, frec, fx_s, fx_r, expert=opposite)
    last.start()
    hg_ref[0] = total - going

    for copy in to_other:
        copy.wait_recv()
    for slab in range(z.nx):
        pair = [hbuf[2 * slab + h].astype(F32) for h in range(2)]
        for side in range(2):
            piece = jnp.concatenate([p[side * z.half : (side + 1) * z.half] for p in pair], axis=0)
            hall[slab, :, side * piece.shape[1] : (side + 1) * piece.shape[1]] = piece.astype(BF16)
    rows_all = dbuf[...].reshape(z.nx * z.rows, dbuf.shape[2])
    tile = min(256, gd_ref.shape[1])

    def columns(n, carry):
        at = pl.ds(pl.multiple_of(n * tile, tile), tile)
        kept = hall[:, :, at].reshape(z.nx * z.rows, tile)
        full = lax.dot_general(
            rows_all, kept, (((0,), (0,)), ((), ())), preferred_element_type=F32
        )
        gd_ref[:, at] = full[:width].astype(BF16)
        return carry

    lax.fori_loop(0, gd_ref.shape[1] // tile, columns, 0)

    last.wait_recv()
    came = frec[...].astype(F32)
    empty = jnp.zeros((z.half - few, came.shape[1]), F32)
    hg_ref[1] = jnp.concatenate([came[:few], empty, came[few:], empty], axis=0)

    for copy in [to_partner] + to_z + to_other + [last]:
        copy.wait_send()
    for step in range(z.nx):
        sent = sbuf.at[step] if step else sbuf.at[0, pl.ds(0, z.slab - 1)]
        send(sent, sent, dx_s.at[step], dx_r.at[step], dp=other).wait_send()
    for q in range(per_half):
        send(pbuf.at[q], prec.at[q], py_s.at[q], py_r.at[q], dp=other).wait_send()
    for k in range(1, z.nz):
        send(ssend.at[0], zrec.at[0], rz_s.at[k], rz_r.at[k], dp=at_z(k)).wait_send()


def hidden_of(stored):
    width = stored.shape[-1] // 2
    gate_part = stored[..., :width].astype(F32)
    up_part = stored[..., width:].astype(F32)
    return (gate_part * jax.nn.sigmoid(gate_part) * up_part).astype(BF16)


def swiglu_back(hidden_grad, stored):
    width = stored.shape[-1] // 2
    gate_part = stored[..., :width].astype(F32)
    up_part = stored[..., width:].astype(F32)
    sigmoid_v = jax.nn.sigmoid(gate_part)
    gate_grad = hidden_grad * up_part * sigmoid_v * (1.0 + gate_part * (1.0 - sigmoid_v))
    up_grad = hidden_grad * gate_part * sigmoid_v
    return jnp.concatenate([gate_grad, up_grad], axis=-1).astype(BF16)


def on_device(z, out_grad, gate_weight, expert_ids, replicated, down_weight, pre_act):
    tokens, width = out_grad.shape
    hidden_width = pre_act.shape[3] // 2
    half_lanes = hidden_width // 2
    myself = lax.axis_index("expert")

    experts = jnp.arange(z.experts, dtype=jnp.int32)
    names = jnp.swapaxes(expert_ids, 0, 1)[None] == experts[:, None, None]
    named = jnp.any(names, axis=1)
    gates = jnp.sum(jnp.where(names, jnp.swapaxes(gate_weight, 0, 1)[None], 0.0), axis=1)
    order = jnp.arange(tokens)
    earlier = (order[:, None] < order[None, :]).astype(BF16)
    ranks = 1.0 + jnp.dot(named.astype(BF16), earlier, preferred_element_type=F32)
    ranks = jnp.where(named, ranks, 0.0)
    high = lax.reduce_precision(gates, 8, 7)
    middle = lax.reduce_precision(gates - high, 8, 7)
    wants = packed_wants(tokens, width)
    blocks, message_rows = packing(width)
    table = jnp.tile(jnp.stack([ranks, high, middle, gates - high - middle]), (1, 1, blocks + 2))
    table = jnp.pad(table, ((0, 0), (0, 0), (0, wants.shape[1] - table.shape[2])))
    table = table.reshape(4, z.nx, z.slab, wants.shape[1])
    ends = out_grad[:, blocks * LANES :]
    beside = LANES - ends.shape[1]
    picks = [out_grad[:, b * LANES : (b + 1) * LANES] for b in range(blocks)]
    picks += [jnp.pad(ends, ((0, 0), (0, beside))), jnp.pad(ends, ((0, 0), (beside, 0)))]
    picks = jnp.concatenate(picks)
    picks = jnp.pad(picks, ((0, wants.shape[1] - picks.shape[0]), (0, 0)))

    hidden = hidden_of(pre_act[0]).reshape(2, z.per_share, CAP, hidden_width)
    hidden = jnp.concatenate([hidden[:, n] for n in share_order(z)], axis=1)
    hidden = jnp.pad(hidden, ((0, 0), (0, z.half - z.share_rows), (0, 0)))
    hidden = hidden.reshape(2, z.half, 2, half_lanes).swapaxes(1, 2).reshape(2, z.rows, half_lanes)
    odd_rows = z.per_share // 2 * CAP
    inside = jnp.arange(z.rows) % z.half
    moved = (inside < odd_rows) & (replicated[myself] == 1)
    moved = jnp.broadcast_to(moved.astype(F32)[:, None], (z.rows, LANES))
    weight = jnp.swapaxes(down_weight[0], 0, 1)
    take = jnp.asarray(unpacking(z, width), BF16)
    few = (2 * up_to(odd_rows, 8), half_lanes)

    chunk = (z.rows, half_lanes)
    dma = pltpu.SemaphoreType.DMA
    gd, hg = pl.pallas_call(
        functools.partial(kernel, z),
        out_shape=(
            jax.ShapeDtypeStruct((width, hidden_width), BF16),
            jax.ShapeDtypeStruct((2,) + chunk, F32),
        ),
        in_specs=[pl.BlockSpec(memory_space=pltpu.VMEM)] * 7,
        out_specs=(pl.BlockSpec(memory_space=pltpu.VMEM),) * 2,
        scratch_shapes=[
            pltpu.VMEM((z.nx, z.slab, message_rows, LANES), BF16),
            pltpu.VMEM((z.nx, z.slab, message_rows, LANES), BF16),
            pltpu.VMEM(chunk, BF16),
            pltpu.VMEM((z.dp,) + chunk, BF16),
            pltpu.VMEM((z.nx, z.rows, hidden_width), BF16),
            pltpu.VMEM((z.nx, z.rows, up_to(width, LANES)), BF16),
            pltpu.VMEM((z.nx, 2) + chunk, BF16),
            pltpu.VMEM((z.nx // 2, 2) + chunk, BF16),
            pltpu.VMEM((z.nz,) + chunk, BF16),
            pltpu.VMEM((z.nz,) + chunk, BF16),
            pltpu.VMEM(few, BF16),
            pltpu.VMEM(few, BF16),
            dma, dma,
            dma((z.nz,)), dma((z.nz,)), dma((z.nz,)), dma((z.nz,)),
            dma((z.nx,)), dma((z.nx,)), dma((z.nx // 2,)), dma((z.nx // 2,)),
            dma((z.nz,)), dma((z.nz,)), dma, dma,
        ],
        compiler_params=pltpu.CompilerParams(
            collective_id=0, has_side_effects=True, vmem_limit_bytes=40 << 20
        ),
    )(picks, table, hidden, moved, jnp.asarray(wants), take, weight)

    hg = hg.reshape(2, 2, z.half, half_lanes)[:, :, : z.share_rows]
    hg = hg.reshape(2, 2, z.per_share, CAP, half_lanes)
    placed = share_order(z)
    hg = jnp.concatenate([hg[:, :, placed.index(n)] for n in range(z.per_share)], axis=2)
    hg = hg.swapaxes(1, 2).reshape(2, z.share_rows, hidden_width)
    return (jnp.swapaxes(gd, 0, 1)[None], swiglu_back(hg, pre_act[0])[None])


def solution(mesh):
    in_specs = (
        P("expert", "dp"),
        P("expert", None),
        P("expert", None),
        P(),
        P("expert", None, "dp"),
        P("expert", None, "dp", None),
    )
    out_specs = (P("expert", None, "dp"), P("expert", None, "dp", None))
    return jax.shard_map(
        functools.partial(on_device, Sizes(mesh)),
        mesh=mesh, in_specs=in_specs, out_specs=out_specs, check_vma=False,
    )
```

time: 91.1 us -> 85.8 us (0.942)
  Pallas kernels: 82 us -> 74.9 us
  other arithmetic: 2 us -> 3.37 us
    pallas_call x1, Pallas kernels: 82 us -> 74.9 us  [on_device(): pl.pallas_call(functools.partial(kernel, z), out_shape=(jax.ShapeDtypeStr...]
    convert_element_type x1, other arithmetic: 0.35 us -> 1.34 us  [hidden_of(): return (gate_part * jax.nn.sigmoid(gate_part) * up_part).astype(BF16)]
    unnamed x17 -> x23, local copies, waits for them, and re-layouts: 3.3 us -> 4.16 us
where the time goes in v3:
time: 85.8 us; the launch traced here: 85.5 us
  Pallas kernels  74.9 us (87%)
  local copies, waits for them, and re-layouts  5.51 us (6%)
  other arithmetic  3.37 us (4%)
  between operations  1.54 us (2%)
    pallas_call x1, Pallas kernels, on_device(): pl.pallas_call(functools.partial(kernel, z), out_shape=(jax.ShapeDtypeStr...  74.9 us
    unnamed x23, local copies, waits for them, and re-layouts  4.16 us

profile of v3, /device:TPU:128, one launch (start us, length us, event | category | flops | bytes accessed | tf_op | source)
XLA Modules:
  0.0 85.5 jit_solution(6180201324989347880)
XLA Ops:
  0.6 1.3 %fusion.6 = (bf16[2,36,1024]{2,0,1:T(2,128)(2,1)S(1)}, f32[2,36,1024]{2,0,1:T(2,128)S(1)}) fusion(bf16[2,36,2048]{2,0,1:T(2,128)(2,1)} %bitcast.69), kind=kLoop, calls=%fused_computation.14 | loop fusion | flops 589824 | bytes 737280 | tf_op jit(solution)/shard_map/convert_element_type | solution.py:265
  2.0 0.1 fusion.25
  2.1 0.1 fusion.19
  2.2 0.1 reshape.102
  2.3 0.0 copy-start.6
  2.4 0.0 copy-start.5
  2.4 0.6 copy-done.6
  3.0 0.0 copy-done.5
  3.1 0.2 select_reduce_fusion
  3.3 0.1 fusion.16
  3.4 0.2 fusion.1
  3.6 0.0 copy-start
  3.7 0.2 copy.58
  3.8 0.0 copy-start.7
  3.9 0.0 copy-start.4
  3.9 0.0 copy-start.1
  3.9 0.7 copy-done.7
  4.6 0.6 dynamic_slice.3
  5.8 0.1 broadcast_in_dim.34.moved_ref
  5.9 0.0 copy-done.4
  6.0 0.1 pad_dynamic-update-slice_fusion
  6.1 0.0 copy-start.2
  6.1 0.0 copy-done
  6.1 0.0 copy-done.1
  6.1 0.7 copy-done.2
  6.8 74.9 %shard_map.95 = (bf16[448,1024]{1,0:T(8,128)(2,1)S(1)}, f32[2,80,512]{2,1,0:T(8,128)S(1)}) custom-call(bf16[256,128]{1,0:T(8,128)(2,1)S(1)} %pad.22.tok_ref, f32[4,8,8,256]{3,2,1,0:T(8,128)S(1)} %pad_bitcast_fusion.tab_ref, bf16[2,80,512]{2,1,0:T(8,128)(2,1)S(1)} %bitcast.65, f32[80,128]{1,0:T(8,128)S(1)} %broadcast_in_dim.34.moved_ref, ...), custom_call_target="tpu_custom_call" | custom-call | tf_op jit(solution)/shard_map/pallas_call | solution.py:320
  81.7 0.2 copy.54
  82.0 0.1 maximum_bitcast_fusion
  82.1 0.0 copy-start.3
  82.2 0.3 reshape.107
  82.4 0.7 copy-done.3
  83.1 0.5 fusion.21
  83.6 1.0 %pad_maximum_fusion = bf16[1,2,36,2048]{3,1,2,0:T(2,128)(2,1)} fusion(bf16[1,2,36,1024]{3,1,2,0:T(2,128)(2,1)S(1)} %get-tuple-element.9, bf16[1,2,36,1024]{3,1,2,0:T(2,128)(2,1)S(1)} %get-tuple-element.8), kind=kLoop, calls=%fused_computation.25 | loop fusion | flops 589824 | bytes 589824 | tf_op jit(solution)/shard_map/concatenate | solution.py:275
  84.6 0.9 %copy.74 = bf16[1,1024,448]{1,2,0:T(8,128)(2,1)} copy(bf16[1,1024,448]{1,2,0:T(8,128)(2,1)S(1)} %bitcast.64) | data formatting | bytes 1835008
  (15 shorter events, 0.2 us)
Async XLA Ops:
  2.3 0.7 copy-start.6
  2.4 0.7 copy-start.5
  3.6 2.4 %copy-start = (bf16[1,1024,448]{1,2,0:T(8,128)(2,1)S(1)}, bf16[1,1024,448]{1,2,0:T(8,128)(2,1)}, u32[]{:S(2)}) copy-start(bf16[1,1024,448]{1,2,0:T(8,128)(2,1)} %param.12) | copy-start | bytes 2752516
  3.8 0.7 copy-start.7
  3.9 2.0 %copy-start.4 = (bf16[48,448]{1,0:T(8,128)(2,1)S(1)}, bf16[48,448]{1,0:T(8,128)(2,1)}, u32[]{:S(2)}) copy-start(bf16[48,448]{1,0:T(8,128)(2,1)} %param.8) | copy-start | bytes 129028
  3.9 2.2 %copy-start.1 = (bf16[400,256]{1,0:T(8,128)(2,1)S(1)}, bf16[400,256]{1,0:T(8,128)(2,1)}, u32[]{:S(2)}) copy-start(bf16[400,256]{1,0:T(8,128)(2,1)} %constant.38.clone.take_ref) | copy-start | bytes 614404
  6.1 0.8 copy-start.2
  82.1 1.0 %copy-start.3 = (bf16[1,2,36,2048]{3,1,2,0:T(2,128)(2,1)S(1)}, bf16[1,2,36,2048]{3,1,2,0:T(2,128)(2,1)}, u32[]{:S(2)}) copy-start(bf16[1,2,36,2048]{3,1,2,0:T(2,128)(2,1)} %param.13) | copy-start | bytes 884740

commit v4 on v3

--- a/solution.py
+++ b/solution.py
@@ -70,9 +70,9 @@
 
 def kernel(
     z,
-    tok_ref, tab_ref, hid_ref, moved_ref, wants_ref, take_ref, wt_ref,
+    og_ref, id_ref, gate_ref, rep_ref, hid_ref, wants_ref, spread_ref, take_ref, wt_ref,
     gd_ref, hg_ref,
-    sbuf, abuf, theirs, hbuf, hall, dbuf, pbuf, prec, ssend, zrec, fsend, frec,
+    tok_ref, end_ref, tab_ref, sbuf, abuf, theirs, hbuf, hall, dbuf, pbuf, prec, ssend, zrec, fsend, frec,
     th_s, th_r, hz_s, hz_r, hy_s, hy_r,
     dx_s, dx_r, py_s, py_r, rz_s, rz_r, fx_s, fx_r,
 ):
@@ -97,6 +97,7 @@
         return copy
 
     barrier = pltpu.get_barrier_semaphore()
+
     def greet(**where):
         pl.semaphore_signal(barrier, inc=1, device_id=where, device_id_type=pl.DeviceIdType.MESH)
 
@@ -108,16 +109,41 @@
     for k in range(1, z.nz):
         greet(dp=at_z(k))
     greet(dp=other)
-    pl.semaphore_wait(barrier, z.experts + z.nz - 1)
-
-    to_partner = send(hid_ref.at[1], theirs, th_s, th_r, expert=opposite)
-    to_partner.start()
+    count = og_ref.shape[0]
+    table = (z.experts, count)
+    expert = lax.broadcasted_iota(jnp.int32, table, 0)
+    named, gates = jnp.zeros(table, F32), jnp.zeros(table, F32)
+    for k in range(id_ref.shape[0]):
+        here = jnp.broadcast_to(id_ref[k : k + 1, :], table) == expert
+        named = jnp.where(here, 1.0, named)
+        gates = jnp.where(here, jnp.broadcast_to(gate_ref[k : k + 1, :], table), gates)
+    order = [lax.broadcasted_iota(jnp.int32, (count, count), n) for n in range(2)]
+    earlier = jnp.where(order[0] < order[1], 1.0, 0.0).astype(BF16)
+    ranks = named * (1.0 + jnp.dot(named.astype(BF16), earlier, preferred_element_type=F32))
+    high = gates.astype(BF16)
+    middle = (gates - high.astype(F32)).astype(BF16)
+    low = (gates - high.astype(F32) - middle.astype(F32)).astype(BF16)
+    for n, part in enumerate((ranks.astype(BF16), high, middle, low)):
+        wide = jnp.dot(part, spread_ref[...], preferred_element_type=F32)
+        tab_ref[n] = wide.reshape(tab_ref.shape[1:])
+
+    blocks = og_ref.shape[1] // LANES
+    tok_ref[...] = jnp.zeros_like(tok_ref)
+    end_ref[...] = jnp.zeros_like(end_ref)
+    for b in range(blocks):
+        tok_ref[b * count : (b + 1) * count] = og_ref[:, b * LANES : (b + 1) * LANES]
+    ends = og_ref[:, blocks * LANES :].astype(F32)
+    end_ref[:, : ends.shape[1]] = ends
+    ends = end_ref[...]
+    tok_ref[blocks * count : (blocks + 1) * count] = ends.astype(BF16)
+    ends = pltpu.roll(ends, LANES // 2, 1)
+    tok_ref[(blocks + 1) * count : (blocks + 2) * count] = ends.astype(BF16)
 
     message = sbuf.shape[2:]
     width = wt_ref.shape[0]
     tokens, wants = tok_ref[...], wants_ref[...]
 
-    def prepare(step):
+    def prepare(step, carry):
         x = (my_x + step) % z.nx
         shape = (z.slab,) + wants.shape
         hit = jnp.broadcast_to(tab_ref[0, x][:, None], shape) == wants[None]
@@ -127,11 +153,17 @@
             part = part.reshape(-1, shape[2]).astype(BF16)
             picked = picked + jnp.dot(part, tokens, preferred_element_type=F32)
         sbuf[step] = picked.astype(BF16).reshape(sbuf.shape[1:])
-        return x
+        return carry
+
+    lax.fori_loop(0, z.nx, prepare, 0)
+    pl.semaphore_wait(barrier, z.experts + z.nz - 1)
+
+    to_partner = send(hid_ref.at[1], theirs, th_s, th_r, expert=opposite)
+    to_partner.start()
 
     def to_slab(n, carry):
         step = 1 + (n + z.nx // 2 - 1) % (z.nx - 1)
-        x = prepare(step)
+        x = (my_x + step) % z.nx
 
         def one(j, inner):
             send(
@@ -150,11 +182,15 @@
         return carry
 
     lax.fori_loop(0, z.nx - 1, to_slab, 0)
-    prepare(0)
     lax.fori_loop(1, z.slab, to_own_slab, 0)
     abuf[my_x, yc] = sbuf[0, yc]
 
-    moved = jnp.concatenate([moved_ref[...]] * (hbuf.shape[2] // LANES), axis=1)
+    lane = lax.broadcasted_iota(jnp.int32, rep_ref.shape, 1)
+    has_second = jnp.sum(jnp.where(lane == ex, rep_ref[...], 0), axis=1, keepdims=True)
+    row = lax.broadcasted_iota(jnp.int32, theirs.shape, 0)
+    inside = jnp.where(row < z.half, row, row - z.half)
+    second = jnp.broadcast_to(has_second, theirs.shape) == 1
+    moved = jnp.where((inside < z.per_share // 2 * CAP) & second, 1.0, 0.0)
     to_partner.wait_recv()
     hbuf[dp] = (
         hid_ref[0].astype(F32) * (1.0 - moved) + theirs[...].astype(F32) * moved
@@ -279,38 +315,18 @@
     tokens, width = out_grad.shape
     hidden_width = pre_act.shape[3] // 2
     half_lanes = hidden_width // 2
-    myself = lax.axis_index("expert")
-
-    experts = jnp.arange(z.experts, dtype=jnp.int32)
-    names = jnp.swapaxes(expert_ids, 0, 1)[None] == experts[:, None, None]
-    named = jnp.any(names, axis=1)
-    gates = jnp.sum(jnp.where(names, jnp.swapaxes(gate_weight, 0, 1)[None], 0.0), axis=1)
-    order = jnp.arange(tokens)
-    earlier = (order[:, None] < order[None, :]).astype(BF16)
-    ranks = 1.0 + jnp.dot(named.astype(BF16), earlier, preferred_element_type=F32)
-    ranks = jnp.where(named, ranks, 0.0)
-    high = lax.reduce_precision(gates, 8, 7)
-    middle = lax.reduce_precision(gates - high, 8, 7)
+
     wants = packed_wants(tokens, width)
     blocks, message_rows = packing(width)
-    table = jnp.tile(jnp.stack([ranks, high, middle, gates - high - middle]), (1, 1, blocks + 2))
-    table = jnp.pad(table, ((0, 0), (0, 0), (0, wants.shape[1] - table.shape[2])))
-    table = table.reshape(4, z.nx, z.slab, wants.shape[1])
-    ends = out_grad[:, blocks * LANES :]
-    beside = LANES - ends.shape[1]
-    picks = [out_grad[:, b * LANES : (b + 1) * LANES] for b in range(blocks)]
-    picks += [jnp.pad(ends, ((0, 0), (0, beside))), jnp.pad(ends, ((0, 0), (beside, 0)))]
-    picks = jnp.concatenate(picks)
-    picks = jnp.pad(picks, ((0, wants.shape[1] - picks.shape[0]), (0, 0)))
+    spread = np.zeros((tokens, wants.shape[1]), np.float32)
+    for b in range(blocks + 2):
+        spread[:, b * tokens : (b + 1) * tokens] = np.eye(tokens)
 
     hidden = hidden_of(pre_act[0]).reshape(2, z.per_share, CAP, hidden_width)
     hidden = jnp.concatenate([hidden[:, n] for n in share_order(z)], axis=1)
     hidden = jnp.pad(hidden, ((0, 0), (0, z.half - z.share_rows), (0, 0)))
     hidden = hidden.reshape(2, z.half, 2, half_lanes).swapaxes(1, 2).reshape(2, z.rows, half_lanes)
     odd_rows = z.per_share // 2 * CAP
-    inside = jnp.arange(z.rows) % z.half
-    moved = (inside < odd_rows) & (replicated[myself] == 1)
-    moved = jnp.broadcast_to(moved.astype(F32)[:, None], (z.rows, LANES))
     weight = jnp.swapaxes(down_weight[0], 0, 1)
     take = jnp.asarray(unpacking(z, width), BF16)
     few = (2 * up_to(odd_rows, 8), half_lanes)
@@ -323,9 +339,12 @@
             jax.ShapeDtypeStruct((width, hidden_width), BF16),
             jax.ShapeDtypeStruct((2,) + chunk, F32),
         ),
-        in_specs=[pl.BlockSpec(memory_space=pltpu.VMEM)] * 7,
+        in_specs=[pl.BlockSpec(memory_space=pltpu.VMEM)] * 9,
         out_specs=(pl.BlockSpec(memory_space=pltpu.VMEM),) * 2,
         scratch_shapes=[
+            pltpu.VMEM((wants.shape[1], LANES), BF16),
+            pltpu.VMEM((tokens, LANES), F32),
+            pltpu.VMEM((4, z.nx, z.slab, wants.shape[1]), F32),
             pltpu.VMEM((z.nx, z.slab, message_rows, LANES), BF16),
             pltpu.VMEM((z.nx, z.slab, message_rows, LANES), BF16),
             pltpu.VMEM(chunk, BF16),
@@ -346,7 +365,10 @@
         compiler_params=pltpu.CompilerParams(
             collective_id=0, has_side_effects=True, vmem_limit_bytes=40 << 20
         ),
-    )(picks, table, hidden, moved, jnp.asarray(wants), take, weight)
+    )(
+        out_grad, jnp.swapaxes(expert_ids, 0, 1), jnp.swapaxes(gate_weight, 0, 1), replicated[None],
+        hidden, jnp.asarray(wants), jnp.asarray(spread, BF16), take, weight,
+    )
 
     hg = hg.reshape(2, 2, z.half, half_lanes)[:, :, : z.share_rows]
     hg = hg.reshape(2, 2, z.per_share, CAP, half_lanes)

time: 85.8 us -> 81.9 us (0.955)
  local copies, waits for them, and re-layouts: 5.51 us -> 3.33 us
    unnamed x23 -> x20, local copies, waits for them, and re-layouts: 4.16 us -> 2.78 us
where the time goes in v4:
time: 81.9 us; the launch traced here: 81.7 us
  Pallas kernels  74.5 us (91%)
  local copies, waits for them, and re-layouts  3.33 us (4%)
  other arithmetic  3.04 us (4%)
    pallas_call x1, Pallas kernels, on_device(): pl.pallas_call(functools.partial(kernel, z), out_shape=(jax.ShapeDtypeStr...  74.5 us
    unnamed x20, local copies, waits for them, and re-layouts  2.78 us

profile of v4, /device:TPU:128, one launch (start us, length us, event | category | flops | bytes accessed | tf_op | source)
XLA Modules:
  0.0 81.7 jit_solution(5057974768557654745)
XLA Ops:
  0.6 1.3 %fusion.4 = (bf16[2,36,1024]{2,0,1:T(2,128)(2,1)S(1)}, f32[2,36,1024]{2,0,1:T(2,128)S(1)}) fusion(bf16[2,36,2048]{2,0,1:T(2,128)(2,1)} %bitcast.52), kind=kLoop, calls=%fused_computation.11 | loop fusion | flops 589824 | bytes 737280 | tf_op jit(solution)/shard_map/convert_element_type | solution.py:301
  2.0 0.0 copy-start
  2.0 0.1 fusion.20
  2.2 0.1 fusion.16
  2.2 0.1 reshape.54
  2.4 0.0 copy-start.1
  2.4 0.0 copy-start.2
  2.4 0.0 copy-start.3
  2.4 0.0 copy-start.4
  2.4 0.0 copy-start.6
  2.4 0.0 copy-start.5
  2.5 0.0 copy-start.7
  2.5 0.7 copy-done
  3.2 0.2 copy-done.1
  3.4 0.0 copy-done.2
  3.4 0.0 copy-done.3
  3.4 0.0 copy-done.4
  3.4 0.0 copy-done.6
  3.4 0.0 copy-done.5
  3.4 0.0 copy-done.7
  3.4 74.5 %shard_map.104 = (bf16[448,1024]{1,0:T(8,128)(2,1)S(1)}, f32[2,80,512]{2,1,0:T(8,128)S(1)}) custom-call(bf16[48,448]{1,0:T(8,128)(2,1)S(1)} %copy-done.2, s32[8,48]{1,0:T(8,128)S(1)} %bitcast.48, f32[8,48]{1,0:T(8,128)S(1)} %bitcast.49, s32[1,64]{1,0:T(1,128)S(1)} %bitcast.50, bf16[2,80,512]{2,1,0:T(8,128)(2,1)S(1)} %bitcast.46, f32[32,256]{1,0:T(8,128)S(1)} %copy-done.3, ...), custom_call_target="tpu_custom_call" | custom-call | tf_op jit(solution)/shard_map/pallas_call | solution.py:336
  77.9 0.2 copy.41
  78.2 0.1 maximum_bitcast_fusion
  78.3 0.0 copy-start.8
  78.3 0.3 reshape.59
  78.6 0.7 copy-done.8
  79.3 0.5 fusion.18
  79.8 1.0 %pad_maximum_fusion = bf16[1,2,36,2048]{3,1,2,0:T(2,128)(2,1)} fusion(bf16[1,2,36,1024]{3,1,2,0:T(2,128)(2,1)S(1)} %get-tuple-element.9, bf16[1,2,36,1024]{3,1,2,0:T(2,128)(2,1)S(1)} %get-tuple-element.8), kind=kLoop, calls=%fused_computation.22 | loop fusion | flops 589824 | bytes 589824 | tf_op jit(solution)/shard_map/concatenate | solution.py:311
  80.8 0.9 %copy.56 = bf16[1,1024,448]{1,2,0:T(8,128)(2,1)} copy(bf16[1,1024,448]{1,2,0:T(8,128)(2,1)S(1)} %bitcast.45) | data formatting | bytes 1835008
  (4 shorter events, 0.1 us)
Async XLA Ops:
  2.0 1.2 %copy-start = (bf16[1,1024,448]{1,2,0:T(8,128)(2,1)S(1)}, bf16[1,1024,448]{1,2,0:T(8,128)(2,1)}, u32[]{:S(2)}) copy-start(bf16[1,1024,448]{1,2,0:T(8,128)(2,1)} %param.13) | copy-start | bytes 2752516
  2.4 1.0 %copy-start.1 = (bf16[400,256]{1,0:T(8,128)(2,1)S(1)}, bf16[400,256]{1,0:T(8,128)(2,1)}, u32[]{:S(2)}) copy-start(bf16[400,256]{1,0:T(8,128)(2,1)} %constant.11.clone.take_ref) | copy-start | bytes 614404
  2.4 1.0 %copy-start.2 = (bf16[48,448]{1,0:T(8,128)(2,1)S(1)}, bf16[48,448]{1,0:T(8,128)(2,1)}, u32[]{:S(2)}) copy-start(bf16[48,448]{1,0:T(8,128)(2,1)} %og_ref.1) | copy-start | bytes 129028
  2.4 1.0 %copy-start.3 = (f32[32,256]{1,0:T(8,128)S(1)}, f32[32,256]{1,0:T(8,128)}, u32[]{:S(2)}) copy-start(f32[32,256]{1,0:T(8,128)} %constant.12.clone.wants_ref) | copy-start | bytes 98308
  2.4 1.0 %copy-start.4 = (bf16[48,256]{1,0:T(8,128)(2,1)S(1)}, bf16[48,256]{1,0:T(8,128)(2,1)}, u32[]{:S(2)}) copy-start(bf16[48,256]{1,0:T(8,128)(2,1)} %constant.13.clone.spread_ref) | copy-start | bytes 73732
  2.4 0.9 %copy-start.6 = (f32[48,8]{0,1:T(8,128)S(1)}, f32[48,8]{0,1:T(8,128)}, u32[]{:S(2)}) copy-start(f32[48,8]{0,1:T(8,128)} %param.10) | copy-start | bytes 4612
  2.4 0.9 %copy-start.5 = (s32[48,8]{0,1:T(8,128)S(1)}, s32[48,8]{0,1:T(8,128)}, u32[]{:S(2)}) copy-start(s32[48,8]{0,1:T(8,128)} %param.11) | copy-start | bytes 4612
  2.5 0.9 %copy-start.7 = (s32[64]{0:T(128)S(1)}, s32[64]{0:T(128)}, u32[]{:S(2)}) copy-start(s32[64]{0:T(128)} %param.12) | copy-start | bytes 772
  78.3 1.0 %copy-start.8 = (bf16[1,2,36,2048]{3,1,2,0:T(2,128)(2,1)S(1)}, bf16[1,2,36,2048]{3,1,2,0:T(2,128)(2,1)}, u32[]{:S(2)}) copy-start(bf16[1,2,36,2048]{3,1,2,0:T(2,128)(2,1)} %param.14) | copy-start | bytes 884740

commit v5 on v4

--- a/solution.py
+++ b/solution.py
@@ -204,25 +204,26 @@
     to_other[0].start()
 
     per_half = z.nx // 2
-    for k in range(0, z.nx // 2 + 1):
-        for step in (k,) if k in (0, z.nx // 2) else (z.nx - k, k):
-            slab = (my_x + step) % z.nx
-            back = (z.nx - step) % z.nx
-            came = abuf.at[slab] if step else abuf.at[slab, pl.ds(0, z.slab - 1)]
-            send(came, came, dx_s.at[back], dx_r.at[back], dp=other).wait_recv()
-            arrived = abuf[slab].reshape(z.slab * message[0], message[1])
-            taken = jnp.dot(take_ref[...], arrived, preferred_element_type=F32)
-            taken = [taken[n * z.rows : (n + 1) * z.rows] for n in range(taken.shape[0] // z.rows)]
-            ends = taken[-2] + pltpu.roll(taken[-1], LANES // 2, 1)
-            dbuf[slab] = jnp.concatenate(taken[:-2] + [ends], axis=1).astype(BF16)
-            part = jnp.dot(dbuf[slab][:, :width], wt_ref[...], preferred_element_type=F32)
-            for h in range(2):
-                pbuf[slab, h] = stacked(part[h * z.half : (h + 1) * z.half]).astype(BF16)
-
-            @pl.when(slab // per_half != y_lo)
-            def _():
-                q = slab % per_half
-                send(pbuf.at[slab], prec.at[q], py_s.at[q], py_r.at[q], dp=other).start()
+    came = abuf.at[my_x, pl.ds(0, z.slab - 1)]
+    send(came, came, dx_s.at[0], dx_r.at[0], dp=other).wait_recv()
+    for n in range(z.nx):
+        slab = ((1 - y_lo) * per_half + n) % z.nx
+
+        @pl.when(slab != my_x)
+        def _():
+            back = (my_x - slab + z.nx) % z.nx
+            send(abuf.at[slab], abuf.at[slab], dx_s.at[back], dx_r.at[back], dp=other).wait_recv()
+
+        arrived = abuf[slab].reshape(z.slab * message[0], message[1])
+        taken = jnp.dot(take_ref[...], arrived, preferred_element_type=F32)
+        taken = [taken[n * z.rows : (n + 1) * z.rows] for n in range(taken.shape[0] // z.rows)]
+        ends = taken[-2] + pltpu.roll(taken[-1], LANES // 2, 1)
+        dbuf[slab] = jnp.concatenate(taken[:-2] + [ends], axis=1).astype(BF16)
+        part = jnp.dot(dbuf[slab][:, :width], wt_ref[...], preferred_element_type=F32)
+        for h in range(2):
+            pbuf[slab, h] = stacked(part[h * z.half : (h + 1) * z.half]).astype(BF16)
+        if n < per_half:
+            send(pbuf.at[slab], prec.at[n], py_s.at[n], py_r.at[n], dp=other).start()
 
     for q in range(per_half):
         send(pbuf.at[q], prec.at[q], py_s.at[q], py_r.at[q], dp=other).wait_recv()

time: 81.9 us -> 80.1 us (0.978)
  the two profiles are of different devices: /device:TPU:128 before, /device:TPU:13 now
where the time goes in v5:
time: 80.1 us; the launch traced here: 79.9 us
  Pallas kernels  72.7 us (91%)
  local copies, waits for them, and re-layouts  3.33 us (4%)
  other arithmetic  3.04 us (4%)
  between operations  0.81 us (1%)
    pallas_call x1, Pallas kernels, on_device(): pl.pallas_call(functools.partial(kernel, z), out_shape=(jax.ShapeDtypeStr...  72.7 us
    unnamed x20, local copies, waits for them, and re-layouts  2.78 us

profile of v5, /device:TPU:13, one launch (start us, length us, event | category | flops | bytes accessed | tf_op | source)
XLA Modules:
  0.0 79.9 jit_solution(6915890071285759348)
XLA Ops:
  0.6 1.3 %fusion.4 = (bf16[2,36,1024]{2,0,1:T(2,128)(2,1)S(1)}, f32[2,36,1024]{2,0,1:T(2,128)S(1)}) fusion(bf16[2,36,2048]{2,0,1:T(2,128)(2,1)} %bitcast.52), kind=kLoop, calls=%fused_computation.11 | loop fusion | flops 589824 | bytes 737280 | tf_op jit(solution)/shard_map/convert_element_type | solution.py:302
  2.0 0.0 copy-start
  2.0 0.1 fusion.20
  2.2 0.1 fusion.16
  2.2 0.1 reshape.54
  2.4 0.0 copy-start.1
  2.4 0.0 copy-start.2
  2.4 0.0 copy-start.3
  2.4 0.0 copy-start.4
  2.4 0.0 copy-start.6
  2.4 0.0 copy-start.5
  2.5 0.0 copy-start.7
  2.5 0.7 copy-done
  3.2 0.2 copy-done.1
  3.4 0.0 copy-done.2
  3.4 0.0 copy-done.3
  3.4 0.0 copy-done.4
  3.4 0.0 copy-done.6
  3.4 0.0 copy-done.5
  3.4 0.0 copy-done.7
  3.4 72.7 %shard_map.104 = (bf16[448,1024]{1,0:T(8,128)(2,1)S(1)}, f32[2,80,512]{2,1,0:T(8,128)S(1)}) custom-call(bf16[48,448]{1,0:T(8,128)(2,1)S(1)} %copy-done.2, s32[8,48]{1,0:T(8,128)S(1)} %bitcast.48, f32[8,48]{1,0:T(8,128)S(1)} %bitcast.49, s32[1,64]{1,0:T(1,128)S(1)} %bitcast.50, bf16[2,80,512]{2,1,0:T(8,128)(2,1)S(1)} %bitcast.46, f32[32,256]{1,0:T(8,128)S(1)} %copy-done.3, ...), custom_call_target="tpu_custom_call" | custom-call | tf_op jit(solution)/shard_map/pallas_call | solution.py:337
  76.1 0.2 copy.41
  76.3 0.1 maximum_bitcast_fusion
  76.5 0.0 copy-start.8
  76.5 0.3 reshape.59
  76.8 0.7 copy-done.8
  77.4 0.5 fusion.18
  77.9 1.0 %pad_maximum_fusion = bf16[1,2,36,2048]{3,1,2,0:T(2,128)(2,1)} fusion(bf16[1,2,36,1024]{3,1,2,0:T(2,128)(2,1)S(1)} %get-tuple-element.9, bf16[1,2,36,1024]{3,1,2,0:T(2,128)(2,1)S(1)} %get-tuple-element.8), kind=kLoop, calls=%fused_computation.22 | loop fusion | flops 589824 | bytes 589824 | tf_op jit(solution)/shard_map/concatenate | solution.py:312
  78.9 0.9 %copy.56 = bf16[1,1024,448]{1,2,0:T(8,128)(2,1)} copy(bf16[1,1024,448]{1,2,0:T(8,128)(2,1)S(1)} %bitcast.45) | data formatting | bytes 1835008
  (4 shorter events, 0.1 us)
Async XLA Ops:
  2.0 1.2 %copy-start = (bf16[1,1024,448]{1,2,0:T(8,128)(2,1)S(1)}, bf16[1,1024,448]{1,2,0:T(8,128)(2,1)}, u32[]{:S(2)}) copy-start(bf16[1,1024,448]{1,2,0:T(8,128)(2,1)} %param.13) | copy-start | bytes 2752516
  2.4 1.0 %copy-start.1 = (bf16[400,256]{1,0:T(8,128)(2,1)S(1)}, bf16[400,256]{1,0:T(8,128)(2,1)}, u32[]{:S(2)}) copy-start(bf16[400,256]{1,0:T(8,128)(2,1)} %constant.11.clone.take_ref) | copy-start | bytes 614404
  2.4 1.0 %copy-start.2 = (bf16[48,448]{1,0:T(8,128)(2,1)S(1)}, bf16[48,448]{1,0:T(8,128)(2,1)}, u32[]{:S(2)}) copy-start(bf16[48,448]{1,0:T(8,128)(2,1)} %og_ref.1) | copy-start | bytes 129028
  2.4 1.0 %copy-start.3 = (f32[32,256]{1,0:T(8,128)S(1)}, f32[32,256]{1,0:T(8,128)}, u32[]{:S(2)}) copy-start(f32[32,256]{1,0:T(8,128)} %constant.12.clone.wants_ref) | copy-start | bytes 98308
  2.4 1.0 %copy-start.4 = (bf16[48,256]{1,0:T(8,128)(2,1)S(1)}, bf16[48,256]{1,0:T(8,128)(2,1)}, u32[]{:S(2)}) copy-start(bf16[48,256]{1,0:T(8,128)(2,1)} %constant.13.clone.spread_ref) | copy-start | bytes 73732
  2.4 0.9 %copy-start.6 = (f32[48,8]{0,1:T(8,128)S(1)}, f32[48,8]{0,1:T(8,128)}, u32[]{:S(2)}) copy-start(f32[48,8]{0,1:T(8,128)} %param.10) | copy-start | bytes 4612
  2.4 0.9 %copy-start.5 = (s32[48,8]{0,1:T(8,128)S(1)}, s32[48,8]{0,1:T(8,128)}, u32[]{:S(2)}) copy-start(s32[48,8]{0,1:T(8,128)} %param.11) | copy-start | bytes 4612
  2.5 0.9 %copy-start.7 = (s32[64]{0:T(128)S(1)}, s32[64]{0:T(128)}, u32[]{:S(2)}) copy-start(s32[64]{0:T(128)} %param.12) | copy-start | bytes 772
  76.5 1.0 %copy-start.8 = (bf16[1,2,36,2048]{3,1,2,0:T(2,128)(2,1)S(1)}, bf16[1,2,36,2048]{3,1,2,0:T(2,128)(2,1)}, u32[]{:S(2)}) copy-start(bf16[1,2,36,2048]{3,1,2,0:T(2,128)(2,1)} %param.14) | copy-start | bytes 884740
